TPU v7x, 128 devices: a whole 4x4x4 slice. The times are simulated.
128 devices in a mesh: rows: 32 (over z, x, core), half: 4 (over y).
Axes of the slice: x: 4, y: 4, z: 4, core: 2. Of those that a mesh axis runs over, the one named last changes fastest.
Arguments:
- pair: bfloat16 [1024, 1024, 128], P('rows', 'half'), may hold values from -6 to 6
- pair_mask: int32 [1024, 1024], P('rows', 'half'), may hold values from 0 to 1, as said below
- gains: float32 [3, 128], replicated, may hold values from 0.1 to 1.9
- w_tri: bfloat16 [128, 640], replicated, may hold values from -0.5 to 0.5
- w_tri_out: bfloat16 [128, 128], replicated, may hold values from -0.5 to 0.5
- w_att: bfloat16 [128, 512], replicated, may hold values from -0.5 to 0.5
- w_bias: bfloat16 [128, 4], replicated, may hold values from -0.5 to 0.5
- w_att_out: bfloat16 [128, 128], replicated, may hold values from -0.5 to 0.5
Outputs:
- updated: bfloat16 [1024, 1024, 128], P('rows', 'half')
Inputs may be any that keep to these rules, and one draw needn't show every extreme that they name: The last tokens of the crop are padding, between 102 and 2 * (102) of them: pair_mask[i, k] is 0 wherever token i or token k is padding. Other pairs may be 0 as well.
All inputs are finite; a program needn't handle non-finite values.
Results may differ from a plain program's by a relative error of at most 0.012.
Values may be sent and summed in bfloat16 or wider, within the bound.
No kernel may reach another device: no remote copies, remote signals or barrier semaphores. Data moves between devices by JAX's collectives and lax.ppermute only.
A program may use at most 128 MiB of HBM per device.

v0:
```python
import math

import jax
import jax.numpy as jnp
from jax import lax
from jax.sharding import PartitionSpec as P


def layer_norm(value, gain, axis):
    center = value - jnp.mean(value, axis=axis, keepdims=True)
    spread = jnp.mean(center * center, axis=axis, keepdims=True)
    return center * lax.rsqrt(spread + 1e-05) * gain


def shards(pair, pair_mask, gains, w_tri, w_tri_out, w_att, w_bias, w_att_out):
    rows_here, cols_here, width = pair.shape
    field = pair.astype(jnp.float32)
    normed = layer_norm(field, gains[0], -1).astype(jnp.bfloat16)
    edges = jnp.einsum(
        "ikc,cd->dik", normed, w_tri[:, : 4 * width], preferred_element_type=jnp.float32
    )
    weight_mask = pair_mask.astype(jnp.float32)
    left_edge = (weight_mask * jax.nn.sigmoid(edges[width : 2 * width]) * edges[:width]).astype(
        jnp.bfloat16
    )
    right_edge = (
        weight_mask * jax.nn.sigmoid(edges[3 * width :]) * edges[2 * width : 3 * width]
    ).astype(jnp.bfloat16)
    gate_field = jax.nn.sigmoid(
        jnp.einsum("ikc,cd->ikd", normed, w_tri[:, 4 * width :], preferred_element_type=jnp.float32)
    )
    left_all, right_all = (
        lax.all_to_all(left_edge, "rows", split_axis=0, concat_axis=1, tiled=True),
        lax.all_to_all(right_edge, "rows", split_axis=0, concat_axis=1, tiled=True),
    )
    product = lax.psum_scatter(
        jnp.einsum("cik,cjk->jci", left_all, right_all, preferred_element_type=jnp.float32).astype(
            jnp.bfloat16
        ),
        "half",
        scatter_dimension=0,
        tiled=True,
    )
    returned = lax.all_to_all(product, "rows", split_axis=2, concat_axis=1, tiled=True)
    tri_normed = layer_norm(returned.astype(jnp.float32), gains[1][:, None], 1).astype(jnp.bfloat16)
    update = jnp.einsum("jci,cd->ijd", tri_normed, w_tri_out, preferred_element_type=jnp.float32)
    after_mult = (field + gate_field * update).astype(jnp.bfloat16)
    att_normed = layer_norm(after_mult.astype(jnp.float32), gains[2], -1).astype(jnp.bfloat16)
    projected = jnp.einsum(
        "ijc,cd->ijd", att_normed, w_att, preferred_element_type=jnp.float32
    ).astype(jnp.bfloat16)
    queries = projected[..., :width]
    keys_here = projected[..., width : 2 * width]
    values_here = projected[..., 2 * width : 3 * width]
    gate_attn = projected[..., 3 * width :]
    bias_local = jnp.einsum(
        "ijc,ch->hij", att_normed, w_bias, preferred_element_type=jnp.float32
    ).astype(jnp.bfloat16)
    bias_rows = lax.all_gather(bias_local, "rows", axis=1, tiled=True)
    bias_full = lax.all_gather(bias_rows, "half", axis=2, tiled=True)
    bias_mine = lax.dynamic_slice_in_dim(
        bias_full, lax.axis_index("half") * cols_here, cols_here, 1
    )
    heads = w_bias.shape[1]
    head_dim = width // heads
    scale = head_dim ** (-0.5)
    group = math.gcd(rows_here, 4)
    blocks = rows_here // group
    query_groups = queries.reshape(blocks, group, cols_here, heads, head_dim)
    mask_wire = pair_mask.astype(jnp.bfloat16)
    piece_keys = lax.all_gather(keys_here, "half", axis=1, tiled=True)
    piece_values = lax.all_gather(values_here, "half", axis=1, tiled=True)
    piece_mask = lax.all_gather(mask_wire, "half", axis=1, tiled=True)
    span = piece_keys.shape[1]
    bias_piece = bias_mine.astype(jnp.float32)
    key_groups = piece_keys.reshape(blocks, group, span, heads, head_dim)
    value_groups = piece_values.reshape(blocks, group, span, heads, head_dim)
    mask_groups = piece_mask.astype(jnp.float32).reshape(blocks, group, span)

    def one_block(items):
        query_block, key_block, value_block, mask_block, running, peak, denom = items
        scores = (
            jnp.einsum(
                "gjhd,gkhd->ghjk", query_block, key_block, preferred_element_type=jnp.float32
            )
            * scale
        )
        scores = scores + bias_piece[None]
        scores = jnp.where(mask_block[:, None, None, :] > 0.5, scores, -1000000000.0)
        new_peak = jnp.maximum(peak, jnp.max(scores, axis=-1))
        shrink = jnp.exp(peak - new_peak)
        weights = jnp.exp(scores - new_peak[..., None])
        denom = denom * shrink + jnp.sum(weights, axis=-1)
        running = running * shrink[..., None] + jnp.einsum(
            "ghjk,gkhd->ghjd",
            weights.astype(jnp.bfloat16),
            value_block,
            preferred_element_type=jnp.float32,
        )
        return (running, new_peak, denom)

    running = jnp.zeros((blocks, group, heads, cols_here, head_dim), jnp.float32)
    peak = jnp.full((blocks, group, heads, cols_here), -1e30, jnp.float32)
    denom = jnp.zeros((blocks, group, heads, cols_here), jnp.float32)
    running, peak, denom = lax.map(
        one_block, (query_groups, key_groups, value_groups, mask_groups, running, peak, denom)
    )
    attended = (running / denom[..., None]).reshape(rows_here, heads, cols_here, head_dim)
    attended = jnp.transpose(attended, (0, 2, 1, 3)).reshape(rows_here, cols_here, width)
    gated = (attended * jax.nn.sigmoid(gate_attn.astype(jnp.float32))).astype(jnp.bfloat16)
    output = jnp.einsum("ijc,cd->ijd", gated, w_att_out, preferred_element_type=jnp.float32)
    return (after_mult.astype(jnp.float32) + output).astype(jnp.bfloat16)


def solution(mesh):
    in_specs = (P("rows", "half", None), P("rows", "half"), P(), P(), P(), P(), P(), P())
    out_specs = P("rows", "half", None)
    return jax.shard_map(shards, mesh=mesh, in_specs=in_specs, out_specs=out_specs, check_vma=False)
```

profile of v0, /device:TPU:100, one launch (start us, length us, event | category | flops | bytes accessed | tf_op | source)
XLA Modules:
  0.0 691.1 jit_solution(11790933083862708372)
XLA Ops:
  21.8 7.2 %all-to-all-start = ((bf16[128,32,256]{2,1,0:T(8,128)(2,1)}), bf16[128,32,256]{2,1,0:T(8,128)(2,1)}, u32[]{:S(2)}, u32[]{:S(2)}) async-start(bf16[128,32,256]{2,1,0:T(8,128)(2,1)} %copy.48), calls=%async_computation | async-start | bytes 4194304 | tf_op jit(solution)/shard_map/all_to_all | solution.py:34
  33.7 19.9 %all-to-all-done = bf16[128,32,256]{2,1,0:T(8,128)(2,1)} async-done(((bf16[128,32,256]{2,1,0:T(8,128)(2,1)}), bf16[128,32,256]{2,1,0:T(8,128)(2,1)}, u32[]{:S(2)}, u32[]{:S(2)}) %all-to-all-start) | async-done | bytes 2097184 | tf_op jit(solution)/shard_map/all_to_all | solution.py:34
  53.6 10.2 %all-to-all-start.1 = ((bf16[128,32,256]{2,1,0:T(8,128)(2,1)}), bf16[128,32,256]{2,1,0:T(8,128)(2,1)}, u32[]{:S(2)}, u32[]{:S(2)}) async-start(bf16[128,32,256]{2,1,0:T(8,128)(2,1)} %copy.50), calls=%async_computation.1 | async-start | bytes 4194304 | tf_op jit(solution)/shard_map/all_to_all | solution.py:33
  67.0 21.8 %all-to-all-done.1 = bf16[128,32,256]{2,1,0:T(8,128)(2,1)} async-done(((bf16[128,32,256]{2,1,0:T(8,128)(2,1)}), bf16[128,32,256]{2,1,0:T(8,128)(2,1)}, u32[]{:S(2)}, u32[]{:S(2)}) %all-to-all-start.1) | async-done | bytes 2097184 | tf_op jit(solution)/shard_map/all_to_all | solution.py:33
  91.0 5.6 convert_bitcast_fusion
  96.7 82.7 %reduce-scatter.2.cloned.1.call-done = bf16[256,4,1024]{2,0,1:T(8,128)(2,1)} async-done(((bf16[1024,4,1024]{2,0,1:T(8,128)(2,1)}), bf16[256,4,1024]{2,0,1:T(8,128)(2,1)}) %reduce-scatter.2.cloned.1.call-update) | async-done | bytes 2097168 | tf_op jit(solution)/shard_map/reduce_scatter | solution.py:36
  183.6 31.8 %all_to_all.45 = bf16[256,4,1024]{0,1,2:T(4,128)(2,1)S(1)} all-to-all(bf16[256,4,1024]{0,1,2:T(4,128)(2,1)} %copy.52), channel_id=1, replica_groups=mesh['rows'=32,'half'=4] {'rows'}, dimensions={2} | all-to-all | bytes 4194304 | tf_op jit(solution)/shard_map/all_to_all | solution.py:44
  224.9 42.1 %all-gather.7.cloned.1.call-done = bf16[4,1024,256]{2,0,1:T(4,128)(2,1)} async-done(((bf16[4,32,256]{2,0,1:T(4,128)(2,1)}), bf16[4,1024,256]{2,0,1:T(4,128)(2,1)}) %all-gather.7.cloned.1.call-update) | async-done | bytes 2097168 | tf_op jit(solution)/shard_map/all_gather | solution.py:59
  276.2 12.6 %all_gather.15 = bf16[32,1024]{1,0:T(8,128)(2,1)S(1)} all-gather(bf16[32,256]{1,0:T(8,128)(2,1)S(1)} %get-tuple-element.101), channel_id=1, replica_groups=mesh['rows'=32,'half'=4] {'half'}, dimensions={1}, use_global_device_ids=true | all-gather | bytes 81920 | tf_op jit(solution)/shard_map/all_gather | solution.py:73
  288.8 68.7 %all-gather.9.cloned.1.call-done = bf16[4,1024,1024]{2,0,1:T(4,128)(2,1)} async-done(((bf16[4,1024,256]{2,0,1:T(4,128)(2,1)}), bf16[4,1024,1024]{2,0,1:T(4,128)(2,1)}) %all-gather.9.cloned.1.call-update) | async-done | bytes 8388624 | tf_op jit(solution)/shard_map/all_gather | solution.py:60
  364.8 82.3 %all-gather.5.cloned.1.call-done = bf16[32,1024,128]{1,2,0:T(8,128)(2,1)} async-done(((bf16[32,256,128]{1,2,0:T(8,128)(2,1)}), bf16[32,1024,128]{1,2,0:T(8,128)(2,1)}) %all-gather.5.cloned.1.call-update) | async-done | bytes 8388624 | tf_op jit(solution)/shard_map/all_gather | solution.py:71
  447.0 89.3 %all-gather.11.cloned.1.call-done = bf16[32,1024,128]{1,2,0:T(8,128)(2,1)} async-done(((bf16[32,256,128]{1,2,0:T(8,128)(2,1)}), bf16[32,1024,128]{1,2,0:T(8,128)(2,1)}) %all-gather.11.cloned.1.call-update) | async-done | bytes 8388624 | tf_op jit(solution)/shard_map/all_gather | solution.py:72
  536.3 138.9 %while.12 = (s32[]{:T(128)}, f32[8,4,4,256,32]{3,4,2,1,0:T(8,128)}, f32[8,4,4,256]{3,2,1,0:T(4,128)S(1)}, f32[8,4,1024]{2,1,0:T(4,128)S(1)}, bf16[8,4,256,4,32]{...) while((s32[]{:T(128)}, f32[8,4,4,256,32]{3,4,2,1,0:T(8,128)}, ...), condition=%wide.region_10.11_spmd, body=%wide.region_7.10_spmd.sunk | while | flops 595746816 | bytes 82790528 | solution.py:105
  536.3 5.8 fusion.83
  542.2 5.0 fusion.85
  547.2 6.6 fusion.84
  553.9 5.6 fusion.83
  559.5 5.0 fusion.85
  564.5 6.6 fusion.84
  571.2 5.7 fusion.83
  582.0 6.6 fusion.84
  588.7 5.5 fusion.83
  599.2 6.6 fusion.84
  605.9 5.5 fusion.83
  616.5 6.6 fusion.84
  623.1 5.7 fusion.83
  633.9 6.6 fusion.84
  640.5 5.6 fusion.83
  646.2 5.0 fusion.85
  651.2 6.7 fusion.84
  657.9 5.6 fusion.83
  668.5 6.7 fusion.84
  (116 shorter events, 90.0 us)
Async XLA Ops:
  6.5 260.5 %copy-start = (bf16[128,512]{1,0:T(8,128)(2,1)S(1)}, bf16[128,512]{1,0:T(8,128)(2,1)}, u32[]{:S(2)}) copy-start(bf16[128,512]{1,0:T(8,128)(2,1)} %param.15) | copy-start | bytes 393220
  6.5 4.4 copy-start.10
  6.5 4.4 copy-start.9
  6.5 4.5 copy-start.7
  21.8 31.8 %all-to-all-start = ((bf16[128,32,256]{2,1,0:T(8,128)(2,1)}), bf16[128,32,256]{2,1,0:T(8,128)(2,1)}, u32[]{:S(2)}, u32[]{:S(2)}) async-start(bf16[128,32,256]{2,1,0:T(8,128)(2,1)} %copy.48), calls=%async_computation | async-start | bytes 4194304 | tf_op jit(solution)/shard_map/all_to_all | solution.py:34
  53.6 35.1 %all-to-all-start.1 = ((bf16[128,32,256]{2,1,0:T(8,128)(2,1)}), bf16[128,32,256]{2,1,0:T(8,128)(2,1)}, u32[]{:S(2)}, u32[]{:S(2)}) async-start(bf16[128,32,256]{2,1,0:T(8,128)(2,1)} %copy.50), calls=%async_computation.1 | async-start | bytes 4194304 | tf_op jit(solution)/shard_map/all_to_all | solution.py:33
  63.8 115.6 %reduce-scatter.2.cloned.1.call-start = ((), (), s32[]{:S(2)}) async-start(), calls=%async_computation.4 | async-start | bytes 10485760 | tf_op jit(solution)/shard_map/reduce_scatter | solution.py:36
  88.8 2.2 copy-start.4
  96.6 170.3 %all-gather.7.cloned.1.call-start = ((), (), s32[]{:S(2)}) async-start(), calls=%async_computation.6 | async-start | bytes 2162688 | tf_op jit(solution)/shard_map/all_gather | solution.py:59
  217.5 0.8 copy-start.8
  219.9 3.5 copy-start.12
  222.1 1.3 copy-start.5
  224.8 132.7 %all-gather.9.cloned.1.call-start = ((), (), s32[]{:S(2)}) async-start(), calls=%async_computation.7 | async-start | bytes 10485760 | tf_op jit(solution)/shard_map/all_gather | solution.py:60
  267.0 180.1 %all-gather.5.cloned.1.call-start = ((), (), s32[]{:S(2)}) async-start(), calls=%async_computation.5 | async-start | bytes 10485760 | tf_op jit(solution)/shard_map/all_gather | solution.py:71
  271.1 4.5 copy-start.3
  275.6 260.8 %all-gather.11.cloned.1.call-start = ((), (), s32[]{:S(2)}) async-start(), calls=%async_computation.8 | async-start | bytes 10485760 | tf_op jit(solution)/shard_map/all_gather | solution.py:72
  536.3 5.9 copy-start.2
  553.9 5.7 copy-start.2
  571.2 5.8 copy-start.2
  588.6 5.6 copy-start.2
  605.9 5.6 copy-start.2
  623.1 5.8 copy-start.2
  640.5 5.7 copy-start.2
  657.9 5.6 copy-start.2
  675.2 3.2 copy-start.6
  675.2 3.3 copy-start.11
  678.5 6.1 copy-start.1
Sparse Core Ops, SparseCore 0:
  96.7 82.6 reduce-scatter.1
  225.0 41.9 all-gather.6
  268.6 88.8 all-gather.8
  359.0 87.9 all-gather.4
  448.5 87.7 all-gather.10
where the time goes:
time: 693 us; the launch traced here: 691 us
  waiting for transfers between devices  407 us (59%)
  matrix products  119 us (17%)
  other arithmetic  54.1 us (8%)
  blocking collectives  44.4 us (6%)
  local copies, waits for them, and re-layouts  35.1 us (5%)
  starting transfers between devices  17.6 us (3%)
  between operations  13.4 us (2%)
    all_gather x1, waiting for transfers between devices, shards(): piece_values = lax.all_gather(values_here, 'half', axis=1, tiled=True)  89.3 us
    reduce_scatter x1, waiting for transfers between devices, shards(): lax.psum_scatter(jnp.einsum('cik,cjk->jci', left_all, right_all, preferre...  82.7 us
    all_gather x1, waiting for transfers between devices, shards(): piece_keys = lax.all_gather(keys_here, 'half', axis=1, tiled=True)  82.3 us
    all_gather x1, waiting for transfers between devices, shards(): bias_full = lax.all_gather(bias_rows, 'half', axis=2, tiled=True)  68.7 us
    dot_general x8, matrix products, one_block(): jnp.einsum('ghjk,gkhd->ghjd', weights.astype(jnp.bfloat16), value_block,...  53.1 us
    dot_general x8, matrix products, one_block(): jnp.einsum('gjhd,gkhd->ghjk', query_block, key_block, preferred_element_t...  45.2 us
    all_gather x1, waiting for transfers between devices, shards(): bias_rows = lax.all_gather(bias_local, 'rows', axis=1, tiled=True)  42.1 us
    reduce_sum x8, other arithmetic, one_block(): denom = denom * shrink + jnp.sum(weights, axis=-1)  39.8 us
  transfers between devices with their start and end apart: 7, of which 7 were waited for; matrix products, arithmetic and copies ran while one was open for 3% of the time, Pallas kernels for 0%

commit v1 on v0

v1 whole, which is shorter than its diff:
```python
import functools

import jax
import jax.numpy as jnp
from jax import lax
from jax.experimental import pallas as pl
from jax.experimental.pallas import tpu as pltpu
from jax.sharding import PartitionSpec as P

LOG2E = 1.4426950408889634
NEG = -1e30
SAFE = 100.0
AXES = ("rows", "half")
VMEM = pl.BlockSpec(memory_space=pltpu.VMEM)


def dot_nn(a, b):
    return lax.dot_general(a, b, (((1,), (0,)), ((), ())), preferred_element_type=jnp.float32)


def dot_nt(a, b):
    return lax.dot_general(a, b, (((1,), (1,)), ((), ())), preferred_element_type=jnp.float32)


def dot_tn(a, b):
    return lax.dot_general(a, b, (((0,), (0,)), ((), ())), preferred_element_type=jnp.float32)


def layer_norm(value, gain, axis):
    center = value - jnp.mean(value, axis=axis, keepdims=True)
    spread = jnp.mean(center * center, axis=axis, keepdims=True)
    return center * lax.rsqrt(spread + 1e-05) * gain


def edges_kernel(pair_ref, mask_ref, gain_ref, wt_ref, out_ref, scr):
    group, cols, width = pair_ref.shape
    gain = gain_ref[0:1, :]

    def row(i, carry):
        x = pair_ref[i].astype(jnp.float32)
        normed = layer_norm(x, gain, -1).astype(jnp.bfloat16)
        mixed = dot_nt(wt_ref[...], normed)
        m = mask_ref[pl.ds(i, 1), :]
        left = m * jax.nn.sigmoid(mixed[width : 2 * width]) * mixed[:width]
        right = m * jax.nn.sigmoid(mixed[3 * width :]) * mixed[2 * width : 3 * width]
        for e, edge in enumerate((left, right)):
            for s in range(cols // 128):
                scr[e, s, pl.ds(i, width, stride=group), :] = edge[:, s * 128 : (s + 1) * 128]
        return carry

    lax.fori_loop(0, group, row, 0, unroll=2)
    for e in range(2):
        for s in range(cols // 128):
            out_ref[:, e, :, s * 128 : (s + 1) * 128] = (
                scr[e, s].reshape(width, group, 128).astype(jnp.bfloat16)
            )


def edges(pair, mask, gains, wt, group=16):
    rows, cols, width = pair.shape
    return pl.pallas_call(
        edges_kernel,
        grid=(rows // group,),
        out_shape=jax.ShapeDtypeStruct((width, 2, rows, cols), jnp.bfloat16),
        in_specs=[
            pl.BlockSpec((group, cols, width), lambda i: (i, 0, 0)),
            pl.BlockSpec((group, cols), lambda i: (i, 0)),
            VMEM,
            VMEM,
        ],
        out_specs=pl.BlockSpec((width, 2, group, cols), lambda i: (0, 0, i, 0)),
        scratch_shapes=[pltpu.VMEM((2, cols // 128, width * group, 128), jnp.float32)],
        compiler_params=pltpu.CompilerParams(vmem_limit_bytes=48 << 20),
    )(pair, mask, gains, wt)


def product_kernel(lr_ref, out_ref):
    blocks, halves, _, rows, cols = lr_ref.shape
    step = 256 // rows

    def tile(t, carry):
        acc = None
        for h in range(halves):
            left = lr_ref[pl.ds(t * step, step), h, 0].reshape(step * rows, cols)
            right = lr_ref[:, h, 1].reshape(blocks * rows, cols)
            part = dot_nt(left, right)
            acc = part if acc is None else acc + part
        for h in range(halves):
            out_ref[pl.ds(t * step, step), h] = (
                acc[:, h * cols : (h + 1) * cols].reshape(step, rows, cols).astype(jnp.bfloat16)
            )
        return carry

    lax.fori_loop(0, blocks // step, tile, 0)


def product(lr):
    blocks, halves, _, rows, cols = lr.shape
    return pl.pallas_call(
        product_kernel,
        out_shape=jax.ShapeDtypeStruct((blocks, halves, rows, cols), jnp.bfloat16),
        in_specs=[VMEM],
        out_specs=VMEM,
        compiler_params=pltpu.CompilerParams(vmem_limit_bytes=48 << 20),
    )(lr)


def output_kernel(prod_ref, pair_ref, mask_ref, gain_ref, gcol_ref, w4_ref, wo_ref, wb_ref, out_ref, bias_ref, scr):
    width, rows, cols = prod_ref.shape
    heads = bias_ref.shape[1]
    for s in range(cols // 128):
        for c in range(0, width, 16):
            part = prod_ref[c : c + 16, :, s * 128 : (s + 1) * 128].astype(jnp.float32)
            scr[s, c * rows : (c + 16) * rows, :] = part.reshape(16 * rows, 128)

    def row(i, carry):
        x = jnp.concatenate(
            [scr[s, pl.ds(i, width, stride=rows), :] for s in range(cols // 128)], axis=1
        )
        normed = layer_norm(x, gcol_ref[...], 0).astype(jnp.bfloat16)
        update = dot_tn(normed, wo_ref[...])
        p = pair_ref[i].astype(jnp.float32)
        pn = layer_norm(p, gain_ref[0:1, :], -1).astype(jnp.bfloat16)
        gate = jax.nn.sigmoid(dot_nn(pn, w4_ref[...]))
        after = (p + gate * update).astype(jnp.bfloat16)
        out_ref[i] = after
        a = layer_norm(after.astype(jnp.float32), gain_ref[2:3, :], -1).astype(jnp.bfloat16)
        bias = dot_nt(wb_ref[...], a) * LOG2E
        bias_ref[i] = bias[:heads].astype(jnp.bfloat16)
        return carry

    lax.fori_loop(0, rows, row, 0, unroll=2)
    out_ref[rows, : mask_ref.shape[0], :] = mask_ref[...]
    out_ref[rows, mask_ref.shape[0] :, :] = jnp.zeros_like(out_ref[rows, mask_ref.shape[0] :, :])


def tri_output(prod, pair, mask_flat, gains, gcol, w4, wo, wb, heads):
    width, rows, cols = prod.shape
    return pl.pallas_call(
        output_kernel,
        out_shape=(
            jax.ShapeDtypeStruct((rows + 1, cols, width), jnp.bfloat16),
            jax.ShapeDtypeStruct((rows, heads, cols), jnp.bfloat16),
        ),
        in_specs=[VMEM] * 8,
        out_specs=(VMEM, VMEM),
        scratch_shapes=[pltpu.VMEM((cols // 128, width * rows, 128), jnp.float32)],
        compiler_params=pltpu.CompilerParams(vmem_limit_bytes=48 << 20),
    )(prod, pair, mask_flat, gains, gcol, w4, wo, wb)


def attention_kernel(
    halves, me_ref, bias_ref, gain_ref, wqg_ref, wkv_ref, wo_ref, e_ref, *refs
):
    xs, masks = refs[:halves], refs[halves : 2 * halves]
    out_ref, b32, bmax, mrow, qm, ks, vs, gs, at = refs[2 * halves :]
    i = pl.program_id(0)
    _, cols, width = xs[0].shape
    heads = b32.shape[0]
    hd = width // heads
    lane = lax.broadcasted_iota(jnp.int32, (1, width), 1)
    me = me_ref[0]
    sub = bias_ref.shape[3]

    @pl.when(i == 0)
    def _():
        big = jnp.zeros((8, 128), jnp.float32)
        for s in range(halves):
            kb = lax.rem(me + halves - s, halves)

            def put(t, big):
                for h in range(heads):
                    b = bias_ref[kb, t, h].astype(jnp.float32)
                    b32[h, pl.ds(pl.multiple_of(t * sub, sub), sub), s * cols : (s + 1) * cols] = b
                    big = jnp.maximum(
                        big, jnp.max(jnp.abs(b).reshape(sub // 8, 8, cols // 128, 128), axis=(0, 2))
                    )
                return big

            big = lax.fori_loop(0, bias_ref.shape[1], put, big)
            mrow[s] = masks[s][0, : mrow.shape[1], :].astype(jnp.float32)
            vs[s * cols : (s + 1) * cols, width:] = jnp.ones((cols, width), jnp.bfloat16)
        bmax[0] = jnp.max(big)

    parts = []
    for s in range(halves):
        a = layer_norm(xs[s][0].astype(jnp.float32), gain_ref[2:3, :], -1).astype(jnp.bfloat16)
        kv = dot_nn(a, wkv_ref[...]).astype(jnp.bfloat16)
        ks[s * cols : (s + 1) * cols, :] = kv[:, :width]
        vs[s * cols : (s + 1) * cols, :width] = kv[:, width:]
        parts.append(jnp.max(jnp.abs(kv[:, :width]), axis=0, keepdims=True))
        if s == 0:
            qg = dot_nn(a, wqg_ref[...])
            q = (qg[:, :width] * (LOG2E * hd**-0.5)).astype(jnp.bfloat16)
            gs[...] = jax.nn.sigmoid(qg[:, width:])
            for h in range(heads):
                on = jnp.broadcast_to(lane // hd == h, q.shape)
                qm[h] = jnp.where(on, q, jnp.zeros_like(q))
    kmax = functools.reduce(jnp.maximum, parts).astype(jnp.float32)
    reach = dot_nn((jnp.abs(q).astype(jnp.float32) * kmax).astype(jnp.bfloat16), e_ref[...])
    bound = jnp.max(reach) * 1.02 + bmax[0]
    step = cols // 128
    rows_m = [mrow[s, pl.ds(i * step, step), :] for s in range(halves)]
    mline = jnp.concatenate([r[t : t + 1] for r in rows_m for t in range(step)], axis=1)
    used = jnp.max(mline) > 0.0
    madd = jnp.where(mline > 0.0, 0.0, NEG)

    def attend(shift):
        num = jnp.zeros((cols, width), jnp.float32)
        den = jnp.ones((cols, width), jnp.float32)
        for h in range(heads):
            scores = dot_nt(qm[h], ks[...]) + b32[h] + madd
            if shift:
                scores = scores - jnp.max(scores, axis=-1, keepdims=True)
            weights = jnp.exp2(scores).astype(jnp.bfloat16)
            both = dot_nn(weights, vs[...])
            on = lane // hd == h
            num = jnp.where(on, both[:, :width], num)
            den = jnp.where(on, both[:, width:], den)
        at[...] = num / den

    @pl.when(used & (bound < SAFE))
    def _():
        attend(False)

    @pl.when(used & jnp.logical_not(bound < SAFE))
    def _():
        attend(True)

    @pl.when(jnp.logical_not(used))
    def _():
        mean = jnp.mean(vs[:, :width].astype(jnp.float32), axis=0, keepdims=True)
        at[...] = jnp.broadcast_to(mean, at.shape)

    gated = (at[...] * gs[...]).astype(jnp.bfloat16)
    out = dot_nn(gated, wo_ref[...])
    out_ref[0] = (xs[0][0].astype(jnp.float32) + out).astype(jnp.bfloat16)


def attention(me, bias, gains, wqg, wkv, wo, blocks):
    halves, _, heads, sub, _ = bias.shape
    rows, cols, width = blocks[0].shape
    rows -= 1
    lanes = jnp.arange(width) // (width // heads)
    e = (lanes[:, None] == lanes[None, :]).astype(jnp.bfloat16)
    keys = halves * cols
    step = cols // 128
    return pl.pallas_call(
        functools.partial(attention_kernel, halves),
        grid=(rows,),
        out_shape=jax.ShapeDtypeStruct((rows, cols, width), jnp.bfloat16),
        in_specs=[pl.BlockSpec(memory_space=pltpu.SMEM)]
        + [VMEM] * 6
        + [pl.BlockSpec((1, cols, width), lambda i: (i, 0, 0))] * halves
        + [pl.BlockSpec((1, cols, width), lambda i: (rows, 0, 0))] * halves,
        out_specs=pl.BlockSpec((1, cols, width), lambda i: (i, 0, 0)),
        scratch_shapes=[
            pltpu.VMEM((heads, cols, keys), jnp.float32),
            pltpu.SMEM((1,), jnp.float32),
            pltpu.VMEM((halves, rows * step, 128), jnp.float32),
            pltpu.VMEM((heads, cols, width), jnp.bfloat16),
            pltpu.VMEM((keys, width), jnp.bfloat16),
            pltpu.VMEM((keys, 2 * width), jnp.bfloat16),
            pltpu.VMEM((cols, width), jnp.float32),
            pltpu.VMEM((cols, width), jnp.float32),
        ],
        compiler_params=pltpu.CompilerParams(vmem_limit_bytes=56 << 20),
    )(me, bias, gains, wqg, wkv, wo, e, *blocks, *blocks)


def shards(sizes, pair, pair_mask, gains, w_tri, w_tri_out, w_att, w_bias, w_att_out):
    n_rows, halves = sizes
    rows, cols, width = pair.shape
    heads = w_bias.shape[1]
    mask = pair_mask.astype(jnp.float32)
    lr = edges(pair, mask, gains, w_tri[:, : 4 * width].T)
    lr = lax.all_to_all(lr, AXES, split_axis=0, concat_axis=0, tiled=True)
    prod = product(lr.reshape(n_rows, halves, 2, rows, cols))
    back = lax.all_to_all(
        prod.reshape(width, rows, cols), AXES, split_axis=0, concat_axis=0, tiled=True
    )
    wb = jnp.pad(w_bias.T, ((0, 8 - heads), (0, 0)))
    after, bias = tri_output(
        back,
        pair,
        mask.astype(jnp.bfloat16).reshape(rows * cols // width, width),
        gains,
        gains[1][:, None],
        w_tri[:, 4 * width :],
        w_tri_out,
        wb,
        heads,
    )
    blocks = [after]
    for s in range(1, halves):
        blocks.append(lax.ppermute(after, "half", [(y, (y + s) % halves) for y in range(halves)]))
    inner = n_rows // halves
    swap = [
        ((z * inner + k) * halves + y, (y * inner + k) * halves + z)
        for z in range(halves)
        for k in range(inner)
        for y in range(halves)
    ]
    bias = jnp.swapaxes(bias, 0, 1)
    bias = lax.ppermute(bias, AXES, swap)
    bias = lax.all_gather(bias, "rows", axis=0, tiled=False)
    bias = bias.reshape(halves, inner, heads, rows, cols)
    me = lax.axis_index("half").astype(jnp.int32).reshape(1)
    wqg = jnp.concatenate([w_att[:, :width], w_att[:, 3 * width :]], axis=1)
    wkv = w_att[:, width : 3 * width]
    return attention(me, bias, gains, wqg, wkv, w_att_out, blocks)


def solution(mesh):
    sizes = (mesh.shape["rows"], mesh.shape["half"])
    in_specs = (P("rows", "half", None), P("rows", "half"), P(), P(), P(), P(), P(), P())
    out_specs = P("rows", "half", None)
    return jax.shard_map(
        functools.partial(shards, sizes),
        mesh=mesh,
        in_specs=in_specs,
        out_specs=out_specs,
        check_vma=False,
    )
```

time: 693 us -> 351 us (0.51)
  the two profiles are of different devices: /device:TPU:100 before, /device:TPU:1 now
where the time goes in v1:
time: 351 us; the launch traced here: 350 us
  Pallas kernels  127 us (36%)
  waiting for transfers between devices  123 us (35%)
  blocking collectives  64.8 us (18%)
  starting transfers between devices  14.6 us (4%)
  between operations  13.5 us (4%)
  local copies, waits for them, and re-layouts  5.49 us (2%)
    ppermute x3, waiting for transfers between devices, shards(): lax.ppermute(after, 'half', [(y, (y + s) % halves) for y in range(halves)])  93.8 us
    pallas_call x1, Pallas kernels, attention(): pl.pallas_call(functools.partial(attention_kernel, halves), grid=(rows,),...  86 us
    all_to_all x1, blocking collectives, shards(): lr = lax.all_to_all(lr, AXES, split_axis=0, concat_axis=0, tiled=True)  64.8 us
    all_to_all x1, waiting for transfers between devices, shards(): lax.all_to_all(prod.reshape(width, rows, cols), AXES, split_axis=0, conca...  28.9 us
    pallas_call x1, Pallas kernels, tri_output(): pl.pallas_call(output_kernel, out_shape=(jax.ShapeDtypeStruct((rows + 1,...  21.8 us
    pallas_call x1, Pallas kernels, edges(): pl.pallas_call(edges_kernel, grid=(rows // group,), out_shape=jax.ShapeDt...  12.8 us
    ppermute x3, starting transfers between devices, shards(): lax.ppermute(after, 'half', [(y, (y + s) % halves) for y in range(halves)])  9.08 us
  transfers between devices with their start and end apart: 6, of which 4 were waited for; matrix products, arithmetic and copies ran while one was open for 1% of the time, Pallas kernels for 0%

profile of v1, /device:TPU:1, one launch (start us, length us, event | category | flops | bytes accessed | tf_op | source)
XLA Modules:
  0.0 350.3 jit_solution(10223987760392757356)
XLA Ops:
  6.5 0.8 convert_convert_fusion
  7.3 0.9 slice.18
  8.2 0.1 copy.15
  8.3 0.0 copy-start
  8.3 1.6 copy-done
  9.9 0.7 copy-done.3
  10.6 12.8 %shard_map.82 = bf16[128,2,32,256]{3,2,1,0:T(8,128)(2,1)} custom-call(bf16[32,256,128]{2,1,0:T(8,128)(2,1)S(1)} %copy-done, f32[32,256]{1,0:T(8,128)S(1)} %get-tuple-element.12.mask_ref, f32[3,128]{1,0:T(4,128)S(1)} %copy-done.3, bf16[512,128]{1,0:T(8,128)(2,1)S(1)} %bitcast.9), custom_call_target="tpu_custom_call" | custom-call | tf_op jit(solution)/shard_map/pallas_call | solution.py:61
  23.4 64.8 %all_to_all.10 = bf16[128,2,32,256]{3,2,1,0:T(8,128)(2,1)} all-to-all(bf16[128,2,32,256]{3,2,1,0:T(8,128)(2,1)} %shard_map.82), channel_id=1, replica_groups=mesh['rows'=32,'half'=4] {'rows','half'}, dimensions={0} | all-to-all | bytes 8388608 | tf_op jit(solution)/shard_map/all_to_all | solution.py:277
  88.2 6.5 %shard_map.83 = bf16[32,4,32,256]{3,2,1,0:T(8,128)(2,1)} custom-call(bf16[32,4,2,32,256]{4,3,2,1,0:T(8,128)(2,1)} %bitcast.11), custom_call_target="tpu_custom_call" | custom-call | tf_op jit(solution)/shard_map/pallas_call | solution.py:99
  94.7 4.9 %all-to-all-start.1 = ((bf16[128,32,256]{2,1,0:T(8,128)(2,1)}), bf16[128,32,256]{2,1,0:T(8,128)(2,1)}, u32[]{:S(2)}, u32[]{:S(2)}) async-start(bf16[128,32,256]{2,1,0:T(8,128)(2,1)} %bitcast.3), calls=%async_computation.1 | async-start | bytes 4194304 | tf_op jit(solution)/shard_map/all_to_all | solution.py:279
  99.6 0.0 all-gather.3.cloned.1.call-start
  99.6 0.8 slice.20.w4_ref
  100.4 0.0 copy-done.4
  100.4 0.1 copy.13.gcol_ref
  100.5 0.0 copy-done.7
  100.6 0.0 copy-start.6
  100.6 28.9 %all-to-all-done.1.prod_ref = bf16[128,32,256]{2,1,0:T(8,128)(2,1)} async-done(((bf16[128,32,256]{2,1,0:T(8,128)(2,1)}), bf16[128,32,256]{2,1,0:T(8,128)(2,1)}, u32[]{:S(2)}, u32[]{:S(2)}) %all-to-all-start.1) | async-done | bytes 2097184 | tf_op jit(solution)/shard_map/all_to_all | solution.py:279
  129.5 21.8 %shard_map.84 = (bf16[33,256,128]{2,1,0:T(8,128)(2,1)}, bf16[32,4,256]{2,1,0:T(4,128)(2,1)S(1)}) custom-call(bf16[128,32,256]{2,1,0:T(8,128)(2,1)} %all-to-all-done.1.prod_ref, bf16[32,256,128]{2,1,0:T(8,128)(2,1)S(1)} %copy-done.1, bf16[64,128]{1,0:T(8,128)(2,1)S(1)} %reshape.44.mask_ref, f32[3,128]{1,0:T(4,128)S(1)} %copy-done.4, ...), custom_call_target="tpu_custom_call" | custom-call | tf_op jit(solution)/shard_map/pallas_call | solution.py:139
  151.3 0.7 collective-permute-start
  152.0 0.0 collective-permute-done
  152.0 0.6 copy.14
  152.6 0.0 all-gather.3.cloned.1.call-update
  152.6 8.4 %collective-permute-start.3 = (bf16[33,256,128]{2,1,0:T(8,128)(2,1)}, bf16[33,256,128]{2,1,0:T(8,128)(2,1)S(1)}, u32[]{:S(2)}, u32[]{:S(2)}) collective-permute-start(bf16[33,256,128]{2,1,0:T(8,128)(2,1)} %get-tuple-element.8.refs_0_.refs_4_), channel_id=1, source_target_pairs={{0,3},{1,0},{2,1},{3,2},{4,7},{5,4},{6,5},{7,6},{8,11},{9,8},{10,9... | collective-permute-start | bytes 6488072 | tf_op jit(solution)/shard_map/ppermute | solution.py:296
  161.0 0.0 collective-permute-start.2
  161.0 0.7 collective-permute-start.1
  161.7 0.6 slice.23.wkv_ref
  162.4 0.6 pad_maximum_fusion.wqg_ref
  163.0 0.7 compare_convert_fusion.e_ref
  163.7 43.0 %collective-permute-done.3.refs_3_.refs_7_ = bf16[33,256,128]{2,1,0:T(8,128)(2,1)S(1)} collective-permute-done((bf16[33,256,128]{2,1,0:T(8,128)(2,1)}, bf16[33,256,128]{2,1,0:T(8,128)(2,1)S(1)}, u32[]{:S(2)}, u32[]{:S(2)}) %collective-permute-start.3) | collective-permute-done | bytes 2162720 | tf_op jit(solution)/shard_map/ppermute | solution.py:296
  206.7 2.0 collective-permute-done.2.refs_2_.refs_6_
  208.7 48.8 %collective-permute-done.1.refs_1_.refs_5_ = bf16[33,256,128]{2,1,0:T(8,128)(2,1)} collective-permute-done((bf16[33,256,128]{2,1,0:T(8,128)(2,1)}, bf16[33,256,128]{2,1,0:T(8,128)(2,1)}, u32[]{:S(2)}, u32[]{:S(2)}) %collective-permute-start.1) | collective-permute-done | bytes 2162720 | tf_op jit(solution)/shard_map/ppermute | solution.py:296
  257.5 86.0 %shard_map.85 = bf16[32,256,128]{2,1,0:T(8,128)(2,1)} custom-call(s32[1]{0:T(128)} %bitcast.me_ref, bf16[4,8,4,32,256]{4,3,2,1,0:T(8,128)(2,1)} %bitcast.12, f32[3,128]{1,0:T(4,128)} %gain_ref.5, bf16[128,256]{1,0:T(8,128)(2,1)} %pad_maximum_fusion.wqg_ref, bf16[128,256]{1,0:T(8,128)(2,1)} %slice.23.wkv_ref, bf16[128,128]{1,0:T(8,128)(2,1)} %wo_ref.3, ...), custom_call_target="tpu_custom_call" | custom-call | tf_op jit(solution)/shard_map/pallas_call | solution.py:248
  (16 shorter events, 0.0 us)
Async XLA Ops:
  8.3 1.6 copy-start
  9.9 0.7 copy-start.3
  94.7 5.7 %copy-start.4 = (f32[3,128]{1,0:T(4,128)S(1)}, f32[3,128]{1,0:T(4,128)}, u32[]{:S(2)}) copy-start(f32[3,128]{1,0:T(4,128)} %gain_ref.5) | copy-start | bytes 4612
  94.7 5.8 %copy-start.7 = (bf16[128,4]{0,1:T(4,128)(2,1)S(1)}, bf16[128,4]{0,1:T(4,128)(2,1)}, u32[]{:S(2)}) copy-start(bf16[128,4]{0,1:T(4,128)(2,1)} %param.14) | copy-start | bytes 3076
  94.7 34.8 %copy-start.1 = (bf16[32,256,128]{2,1,0:T(8,128)(2,1)S(1)}, bf16[32,256,128]{2,1,0:T(8,128)(2,1)}, u32[]{:S(2)}) copy-start(bf16[32,256,128]{2,1,0:T(8,128)(2,1)} %pair_ref.3) | copy-start | bytes 6291460
  94.7 34.8 %copy-start.2 = (bf16[128,128]{1,0:T(8,128)(2,1)S(1)}, bf16[128,128]{1,0:T(8,128)(2,1)}, u32[]{:S(2)}) copy-start(bf16[128,128]{1,0:T(8,128)(2,1)} %wo_ref.2) | copy-start | bytes 98308
  94.7 34.8 %all-to-all-start.1 = ((bf16[128,32,256]{2,1,0:T(8,128)(2,1)}), bf16[128,32,256]{2,1,0:T(8,128)(2,1)}, u32[]{:S(2)}, u32[]{:S(2)}) async-start(bf16[128,32,256]{2,1,0:T(8,128)(2,1)} %bitcast.3), calls=%async_computation.1 | async-start | bytes 4194304 | tf_op jit(solution)/shard_map/all_to_all | solution.py:279
  99.6 157.9 %all-gather.3.cloned.1.call-start = ((), (), s32[]{:S(2)}) async-start(), calls=%async_computation.2 | async-start | bytes 2162688 | tf_op jit(solution)/shard_map/all_gather | solution.py:306
  100.6 61.2 %copy-start.6 = (bf16[128,512]{1,0:T(8,128)(2,1)S(1)}, bf16[128,512]{1,0:T(8,128)(2,1)}, u32[]{:S(2)}) copy-start(bf16[128,512]{1,0:T(8,128)(2,1)} %param.13) | copy-start | bytes 393220
  151.3 0.7 collective-permute-start
  152.6 54.0 %collective-permute-start.3 = (bf16[33,256,128]{2,1,0:T(8,128)(2,1)}, bf16[33,256,128]{2,1,0:T(8,128)(2,1)S(1)}, u32[]{:S(2)}, u32[]{:S(2)}) collective-permute-start(bf16[33,256,128]{2,1,0:T(8,128)(2,1)} %get-tuple-element.8.refs_0_.refs_4_), channel_id=1, source_target_pairs={{0,3},{1,0},{2,1},{3,2},{4,7},{5,4},{6,5},{7,6},{8,11},{9,8},{10,9... | collective-permute-start | bytes 6488072 | tf_op jit(solution)/shard_map/ppermute | solution.py:296
  161.0 47.7 %collective-permute-start.2 = (bf16[33,256,128]{2,1,0:T(8,128)(2,1)}, bf16[33,256,128]{2,1,0:T(8,128)(2,1)}, u32[]{:S(2)}, u32[]{:S(2)}) collective-permute-start(bf16[33,256,128]{2,1,0:T(8,128)(2,1)} %get-tuple-element.8.refs_0_.refs_4_), channel_id=1, source_target_pairs={{0,2},{1,3},{2,0},{3,1},{4,6},{5,7},{6,4},{7,5},{8,10},{9,11},{10,... | collective-permute-start | bytes 6488072 | tf_op jit(solution)/shard_map/ppermute | solution.py:296
  161.0 96.5 %collective-permute-start.1 = (bf16[33,256,128]{2,1,0:T(8,128)(2,1)}, bf16[33,256,128]{2,1,0:T(8,128)(2,1)}, u32[]{:S(2)}, u32[]{:S(2)}) collective-permute-start(bf16[33,256,128]{2,1,0:T(8,128)(2,1)} %get-tuple-element.8.refs_0_.refs_4_), channel_id=1, source_target_pairs={{0,1},{1,2},{2,3},{3,0},{4,5},{5,6},{6,7},{7,4},{8,9},{9,10},{10,1... | collective-permute-start | bytes 6488072 | tf_op jit(solution)/shard_map/ppermute | solution.py:296
  206.7 50.9 %copy-start.5 = (bf16[33,256,128]{2,1,0:T(8,128)(2,1)}, bf16[33,256,128]{2,1,0:T(8,128)(2,1)S(1)}, u32[]{:S(2)}) copy-start(bf16[33,256,128]{2,1,0:T(8,128)(2,1)S(1)} %collective-permute-done.3.refs_3_.refs_7_) | copy-start | bytes 6488068
Sparse Core Ops, SparseCore 0:
  152.8 48.8 all-gather.2

commit v2 on v1

v2 whole, which is shorter than its diff:
```python
import functools

import jax
import jax.numpy as jnp
from jax import lax
from jax.experimental import pallas as pl
from jax.experimental.pallas import tpu as pltpu
from jax.sharding import PartitionSpec as P

LOG2E = 1.4426950408889634
NEG = -1e30
SAFE = 100.0
AXES = ("rows", "half")
VMEM = pl.BlockSpec(memory_space=pltpu.VMEM)
SMEM = pl.BlockSpec(memory_space=pltpu.SMEM)
PARAMS = pltpu.CompilerParams(vmem_limit_bytes=52 << 20)
CHUNKS = 2


def dot_nn(a, b):
    return lax.dot_general(a, b, (((1,), (0,)), ((), ())), preferred_element_type=jnp.float32)


def dot_nt(a, b):
    return lax.dot_general(a, b, (((1,), (1,)), ((), ())), preferred_element_type=jnp.float32)


def dot_tn(a, b):
    return lax.dot_general(a, b, (((0,), (0,)), ((), ())), preferred_element_type=jnp.float32)


def sigmoid(x):
    return 0.5 * jnp.tanh(0.5 * x) + 0.5


def averager(width):
    return jnp.full((width, width), 1.0 / width, jnp.bfloat16)


def norm_lanes(x, gain):
    avg = averager(x.shape[-1])
    center = x.astype(jnp.float32) - dot_nn(x, avg)
    spread = dot_nn((center * center).astype(jnp.bfloat16), avg)
    return (center * lax.rsqrt(spread + 1e-05) * gain).astype(jnp.bfloat16)


def norm_sublanes(x, gain):
    avg = averager(x.shape[0])
    center = x.astype(jnp.float32) - dot_nn(avg, x)
    spread = dot_nn(avg, (center * center).astype(jnp.bfloat16))
    return (center * lax.rsqrt(spread + 1e-05) * gain).astype(jnp.bfloat16)


def edges_kernel(pair_ref, mask_ref, gain_ref, wt_ref, out_ref, scr):
    group, cols, width = pair_ref.shape
    gain = gain_ref[0:1, :]

    def row(i, carry):
        normed = norm_lanes(pair_ref[i], gain)
        mixed = dot_nt(wt_ref[...], normed)
        m = mask_ref[pl.ds(i, 1), :]
        left = m * sigmoid(mixed[width : 2 * width]) * mixed[:width]
        right = m * sigmoid(mixed[3 * width :]) * mixed[2 * width : 3 * width]
        for e, edge in enumerate((left, right)):
            for s in range(cols // 128):
                scr[e, s, pl.ds(i, width, stride=group), :] = edge[:, s * 128 : (s + 1) * 128]
        return carry

    lax.fori_loop(0, group, row, 0, unroll=EDGE_UNROLL)
    for e in range(2):
        for s in range(cols // 128):
            out_ref[:, e, :, s * 128 : (s + 1) * 128] = (
                scr[e, s].reshape(width, group, 128).astype(jnp.bfloat16)
            )


EDGE_UNROLL = 4


def edges(pair, mask, gains, wt, group=16):
    rows, cols, width = pair.shape
    return pl.pallas_call(
        edges_kernel,
        grid=(rows // group,),
        out_shape=jax.ShapeDtypeStruct((width, 2, rows, cols), jnp.bfloat16),
        in_specs=[
            pl.BlockSpec((group, cols, width), lambda i: (i, 0, 0)),
            pl.BlockSpec((group, cols), lambda i: (i, 0)),
            VMEM,
            VMEM,
        ],
        out_specs=pl.BlockSpec((width, 2, group, cols), lambda i: (0, 0, i, 0)),
        scratch_shapes=[pltpu.VMEM((2, cols // 128, width * group, 128), jnp.float32)],
        compiler_params=PARAMS,
    )(pair, mask, gains, wt)


def gate_kernel(pair_ref, gain_ref, w4_ref, out_ref):
    for i in range(pair_ref.shape[0]):
        normed = norm_lanes(pair_ref[i], gain_ref[0:1, :])
        out_ref[i] = sigmoid(dot_nn(normed, w4_ref[...])).astype(jnp.bfloat16)


def gate(pair, gains, w4, group=4):
    rows, cols, width = pair.shape
    block = pl.BlockSpec((group, cols, width), lambda i: (i, 0, 0))
    return pl.pallas_call(
        gate_kernel,
        grid=(rows // group,),
        out_shape=jax.ShapeDtypeStruct(pair.shape, jnp.bfloat16),
        in_specs=[block, VMEM, VMEM],
        out_specs=block,
        compiler_params=PARAMS,
        cost_estimate=pl.CostEstimate(
            flops=6 * rows * cols * width * width,
            bytes_accessed=4 * rows * cols * width,
            transcendentals=rows * cols * width,
        ),
    )(pair, gains, w4)


PRODUCT_ROWS = 512


def product_kernel(lr_ref, out_ref):
    blocks, halves, _, rows, cols = lr_ref.shape
    step = PRODUCT_ROWS // rows

    def tile(t, carry):
        acc = None
        for h in range(halves):
            left = lr_ref[pl.ds(t * step, step), h, 0].reshape(step * rows, cols)
            right = lr_ref[:, h, 1].reshape(blocks * rows, cols)
            part = dot_nt(left, right)
            acc = part if acc is None else acc + part
        for h in range(halves):
            out_ref[pl.ds(t * step, step), h] = (
                acc[:, h * cols : (h + 1) * cols].reshape(step, rows, cols).astype(jnp.bfloat16)
            )
        return carry

    lax.fori_loop(0, blocks // step, tile, 0)


def product(lr):
    blocks, halves, _, rows, cols = lr.shape
    return pl.pallas_call(
        product_kernel,
        out_shape=jax.ShapeDtypeStruct((blocks, halves, rows, cols), jnp.bfloat16),
        in_specs=[VMEM],
        out_specs=VMEM,
        compiler_params=PARAMS,
    )(lr)


OUT_UNROLL = 4


def output_kernel(prod_ref, pair_ref, gate_ref, mask_ref, gain_ref, gcol_ref, wo_ref, wb_ref, *refs):
    outs, bias_ref, scr = refs[:CHUNKS], refs[CHUNKS], refs[CHUNKS + 1]
    width, rows, cols = prod_ref.shape
    heads = bias_ref.shape[1]
    per = rows // CHUNKS
    for s in range(cols // 128):
        for c in range(0, width, 16):
            part = prod_ref[c : c + 16, :, s * 128 : (s + 1) * 128].astype(jnp.float32)
            scr[s, c * rows : (c + 16) * rows, :] = part.reshape(16 * rows, 128)

    for c in range(CHUNKS):

        def row(k, carry, c=c):
            i = c * per + k
            x = jnp.concatenate(
                [scr[s, pl.ds(i, width, stride=rows), :] for s in range(cols // 128)], axis=1
            )
            normed = norm_sublanes(x.astype(jnp.bfloat16), gcol_ref[...])
            update = dot_tn(normed, wo_ref[...])
            after = pair_ref[i].astype(jnp.float32) + gate_ref[i].astype(jnp.float32) * update
            after = after.astype(jnp.bfloat16)
            outs[c][k] = after
            a = norm_lanes(after, gain_ref[2:3, :])
            bias = dot_nt(wb_ref[...], a) * LOG2E
            bias_ref[i] = bias[:heads].astype(jnp.bfloat16)
            return carry

        lax.fori_loop(0, per, row, 0, unroll=OUT_UNROLL)
        used = per * cols // width
        outs[c][per, :used, :] = mask_ref[c * used : (c + 1) * used, :]
        outs[c][per, used:, :] = jnp.zeros((cols - used, width), jnp.bfloat16)


def tri_output(prod, pair, gates, mask_flat, gains, gcol, wo, wb, heads):
    width, rows, cols = prod.shape
    part = jax.ShapeDtypeStruct((rows // CHUNKS + 1, cols, width), jnp.bfloat16)
    return pl.pallas_call(
        output_kernel,
        out_shape=(part,) * CHUNKS + (jax.ShapeDtypeStruct((rows, heads, cols), jnp.bfloat16),),
        in_specs=[VMEM] * 8,
        out_specs=(VMEM,) * (CHUNKS + 1),
        scratch_shapes=[pltpu.VMEM((cols // 128, width * rows, 128), jnp.float32)],
        compiler_params=PARAMS,
    )(prod, pair, gates, mask_flat, gains, gcol, wo, wb)


def project_kernel(gain_ref, w_ref, *refs):
    width = gain_ref.shape[1]
    xs = refs[:-5]
    q_ref, g_ref, k_ref, v_ref, m_ref = refs[-5:]
    group, cols, _ = xs[0].shape
    scale = LOG2E * HEAD_DIM**-0.5
    for r in range(group):
        top = None
        for b, x_ref in enumerate(xs):
            a = norm_lanes(x_ref[r], gain_ref[2:3, :])
            at = slice(b * cols, (b + 1) * cols)
            if b == 0:
                mixed = dot_nn(a, w_ref[...])
                q_ref[r] = (mixed[:, :width] * scale).astype(jnp.bfloat16)
                g_ref[r] = sigmoid(mixed[:, 3 * width :]).astype(jnp.bfloat16)
                kv = mixed[:, width : 3 * width].astype(jnp.bfloat16)
            else:
                kv = dot_nn(a, w_ref[:, width : 3 * width]).astype(jnp.bfloat16)
            k_ref[r, at, :] = kv[:, :width]
            v_ref[r, at, :] = kv[:, width:]
            m = jnp.max(jnp.abs(kv[:, :width]), axis=0, keepdims=True).astype(jnp.float32)
            top = m if top is None else jnp.maximum(top, m)
        m_ref[r] = jnp.broadcast_to(top, m_ref.shape[1:])


HEAD_DIM = 32


def project(blocks, gains, w, group=4):
    rows, cols, width = blocks[0].shape
    rows -= 1
    n = len(blocks)
    one = lambda c: pl.BlockSpec((group, c, width), lambda i: (i, 0, 0))
    shape = lambda c: jax.ShapeDtypeStruct((rows, c, width), jnp.bfloat16)
    return pl.pallas_call(
        project_kernel,
        grid=(rows // group,),
        out_shape=(shape(cols), shape(cols), shape(n * cols), shape(n * cols), jax.ShapeDtypeStruct((rows, 8, width), jnp.float32)),
        in_specs=[VMEM, VMEM] + [one(cols)] * n,
        out_specs=(one(cols), one(cols), one(n * cols), one(n * cols), one(8)),
        compiler_params=PARAMS,
        cost_estimate=pl.CostEstimate(
            flops=8 * n * rows * cols * width * width,
            bytes_accessed=8 * n * rows * cols * width,
            transcendentals=rows * cols * width,
        ),
    )(gains, w, *blocks)


def project_last_kernel(gain_ref, w_ref, e_ref, x_ref, q_ref, top_ref, k_ref, v_ref, m_ref):
    width = gain_ref.shape[1]
    for r in range(x_ref.shape[0]):
        a = norm_lanes(x_ref[r], gain_ref[2:3, :])
        kv = dot_nn(a, w_ref[:, width : 3 * width]).astype(jnp.bfloat16)
        k_ref[r] = kv[:, :width]
        v_ref[r] = kv[:, width:]
        m = jnp.max(jnp.abs(kv[:, :width]), axis=0, keepdims=True).astype(jnp.float32)
        top = jnp.maximum(m, top_ref[r, 0:1, :])
        reach = dot_nn((jnp.abs(q_ref[r]).astype(jnp.float32) * top).astype(jnp.bfloat16), e_ref[...])
        m_ref[r] = jnp.broadcast_to(jnp.max(reach, axis=0, keepdims=True), m_ref.shape[1:])


def project_last(block, q, top, gains, w, group=4):
    rows, cols, width = q.shape
    lanes = jnp.arange(width) // HEAD_DIM
    e = (lanes[:, None] == lanes[None, :]).astype(jnp.bfloat16)
    one = lambda c: pl.BlockSpec((group, c, width), lambda i: (i, 0, 0))
    shape = jax.ShapeDtypeStruct((rows, cols, width), jnp.bfloat16)
    return pl.pallas_call(
        project_last_kernel,
        grid=(rows // group,),
        out_shape=(shape, shape, jax.ShapeDtypeStruct((rows, 8, width), jnp.float32)),
        in_specs=[VMEM] * 3 + [one(cols), one(cols), one(8)],
        out_specs=(one(cols), one(cols), one(8)),
        compiler_params=PARAMS,
        cost_estimate=pl.CostEstimate(
            flops=10 * rows * cols * width * width,
            bytes_accessed=8 * rows * cols * width,
            transcendentals=0,
        ),
    )(gains, w, e, block, q, top)


def attention_kernel(halves, me_ref, bias_ref, wo_ref, reach_ref, *refs):
    q_ref, g_ref, x_ref, ka_ref, va_ref, kb_ref, vb_ref = refs[:7]
    masks = refs[7 : 7 + halves]
    out_ref, flags, mrow, vs = refs[7 + halves :]
    i = pl.program_id(0)
    group, cols, width = q_ref.shape
    heads = bias_ref.shape[2]
    lane = lax.broadcasted_iota(jnp.int32, (1, width), 1)
    me = me_ref[0]
    where = [lax.rem(me + s, halves) for s in (0, halves - 1, 1, 2)]
    step = cols // 128
    count = mrow.shape[1] // step

    @pl.when(i == 0)
    def _():
        def big(t, top):
            b = jnp.abs(bias_ref[t // bias_ref.shape[1], lax.rem(t, bias_ref.shape[1])])
            return jnp.maximum(top, b)

        top = lax.fori_loop(
            0, halves * bias_ref.shape[1], big, jnp.zeros(bias_ref.shape[2:], jnp.bfloat16)
        )
        bound = jnp.max(reach_ref[...]) * 1.02 + jnp.max(top.astype(jnp.float32))
        flags[0] = (bound < SAFE).astype(jnp.int32)
        for s in range(halves):
            mrow[s] = masks[s][0, : mrow.shape[1], :].astype(jnp.float32)
        least = None
        seen = jnp.max(mrow[...], axis=0)
        for r in range(count):
            u = jnp.max(seen[r * step : (r + 1) * step], keepdims=True)
            least = u if least is None else jnp.minimum(least, u)
        flags[1] = (jnp.max(least) > 0.0).astype(jnp.int32)
        vs[:, :, width:] = jnp.ones((group, vs.shape[1], width), jnp.bfloat16)

    def mask_line(r):
        at = (i * group + r) * step
        return jnp.concatenate(
            [mrow[s, pl.ds(at + t, 1), :] for s in range(halves) for t in range(step)], axis=1
        )

    def finish(r, attended):
        gated = (attended * g_ref[r].astype(jnp.float32)).astype(jnp.bfloat16)
        return (x_ref[r].astype(jnp.float32) + dot_nn(gated, wo_ref[...])).astype(jnp.bfloat16)

    def attend(shift):
        for r in range(group):
            vs[r, : va_ref.shape[1], :width] = va_ref[r]
            vs[r, va_ref.shape[1] :, :width] = vb_ref[r]
            madd = jnp.where(mask_line(r) > 0.0, 0.0, NEG)
            q = q_ref[r]
            num = jnp.zeros((cols, width), jnp.float32)
            den = jnp.ones((cols, width), jnp.float32)
            for h in range(heads):
                on = lane // (width // heads) == h
                qm = jnp.where(jnp.broadcast_to(on, q.shape), q, jnp.zeros_like(q))
                scores = jnp.concatenate([dot_nt(qm, ka_ref[r]), dot_nt(qm, kb_ref[r])], axis=1)
                bias = jnp.concatenate(
                    [bias_ref[w, :, h].reshape(cols, cols) for w in where], axis=1
                )
                scores = scores + bias.astype(jnp.float32) + madd
                if shift:
                    scores = scores - jnp.max(scores, axis=-1, keepdims=True)
                weights = jnp.exp2(scores).astype(jnp.bfloat16)
                both = dot_nn(weights, vs[r])
                num = jnp.where(on, both[:, :width], num)
                den = jnp.where(on, both[:, width:], den)
            out_ref[r] = finish(r, num / den)

    @pl.when(flags[0] > 0)
    def _():
        attend(False)

    @pl.when(flags[0] == 0)
    def _():
        attend(True)

    @pl.when(flags[1] == 0)
    def _():
        for r in range(group):
            used = jnp.max(mask_line(r), keepdims=True) > 0.0
            mean = jnp.mean(vs[r, :, :width].astype(jnp.float32), axis=0, keepdims=True)
            plain = finish(r, jnp.broadcast_to(mean, (cols, width)))
            out_ref[r] = jnp.where(used, out_ref[r].astype(jnp.float32), plain.astype(jnp.float32)).astype(jnp.bfloat16)


def attention(me, bias, wo, reach, q, g, ka, va, kb, vb, blocks, group=4):
    halves = bias.shape[0]
    rows, cols, width = q.shape
    one = lambda c: pl.BlockSpec((group, c, width), lambda i: (i, 0, 0))
    last = pl.BlockSpec((1, cols, width), lambda i: (rows, 0, 0))
    na, nb = ka.shape[1], kb.shape[1]
    return pl.pallas_call(
        functools.partial(attention_kernel, halves),
        grid=(rows // group,),
        out_shape=jax.ShapeDtypeStruct((rows, cols, width), jnp.bfloat16),
        in_specs=[SMEM, VMEM, VMEM, VMEM]
        + [one(cols)] * 3
        + [one(na), one(na), one(nb), one(nb)]
        + [last] * halves,
        out_specs=one(cols),
        scratch_shapes=[
            pltpu.SMEM((2,), jnp.int32),
            pltpu.VMEM((halves, rows * cols // 128, 128), jnp.float32),
            pltpu.VMEM((group, halves * cols, 2 * width), jnp.bfloat16),
        ],
        compiler_params=PARAMS,
        cost_estimate=pl.CostEstimate(
            flops=8 * rows * 4 * cols * halves * cols * width * 2,
            bytes_accessed=8 * rows * cols * width * halves,
            transcendentals=rows * 4 * cols * cols * halves,
        ),
    )(me, bias, wo, reach, q, g, blocks[0], ka, va, kb, vb, *blocks)


def shards(sizes, pair, pair_mask, gains, w_tri, w_tri_out, w_att, w_bias, w_att_out):
    n_rows, halves = sizes
    rows, cols, width = pair.shape
    heads = w_bias.shape[1]
    mask = pair_mask.astype(jnp.float32)
    lr = edges(pair, mask, gains, w_tri[:, : 4 * width].T)
    lr = lax.all_to_all(lr, AXES, split_axis=0, concat_axis=0, tiled=True)
    gates = gate(pair, gains, w_tri[:, 4 * width :])
    prod = product(lr.reshape(n_rows, halves, 2, rows, cols))
    back = lax.all_to_all(
        prod.reshape(width, rows, cols), AXES, split_axis=0, concat_axis=0, tiled=True
    )
    wb = jnp.pad(w_bias.T, ((0, 8 - heads), (0, 0)))
    mask_flat = mask.astype(jnp.bfloat16).reshape(rows * cols // width, width)
    *after, bias = tri_output(
        back, pair, gates, mask_flat, gains, gains[1][:, None], w_tri_out, wb, heads
    )
    inner = n_rows // halves
    swap = [
        ((z * inner + k) * halves + y, (y * inner + k) * halves + z)
        for z in range(halves)
        for k in range(inner)
        for y in range(halves)
    ]
    bias = jnp.swapaxes(bias, 0, 1)
    bias = lax.ppermute(bias, AXES, swap)
    bias = lax.all_gather(bias, "rows", axis=0, tiled=False)
    bias = bias.reshape(halves, inner, heads, rows, cols)

    up = [(y, (y + 1) % halves) for y in range(halves)]
    down = [(y, (y - 1) % halves) for y in range(halves)]
    parts = []
    for c, own in enumerate(after):
        prev = lax.ppermute(own, "half", up)
        next_ = lax.ppermute(own, "half", down)
        far = lax.ppermute(prev, "half", up) if c % 2 == 0 else lax.ppermute(next_, "half", down)
        parts.append((own, prev, next_, far))
    me = lax.axis_index("half").astype(jnp.int32).reshape(1)
    out = []
    for own, prev, next_, far in parts:
        q, g, ka, va, top = project((own, prev, next_), gains, w_att)
        kb, vb, reach = project_last(far, q, top, gains, w_att)
        out.append(attention(me, bias, w_att_out, reach, q, g, ka, va, kb, vb, (own, prev, next_, far)))
    return jnp.concatenate(out, axis=0)


def solution(mesh):
    sizes = (mesh.shape["rows"], mesh.shape["half"])
    in_specs = (P("rows", "half", None), P("rows", "half"), P(), P(), P(), P(), P(), P())
    out_specs = P("rows", "half", None)
    return jax.shard_map(
        functools.partial(shards, sizes),
        mesh=mesh,
        in_specs=in_specs,
        out_specs=out_specs,
        check_vma=False,
    )
```

time: 351 us -> 351 us (level)
  the two profiles are of different devices: /device:TPU:1 before, /device:TPU:100 now
where the time goes in v2:
time: 351 us; the launch traced here: 346 us
  Pallas kernels  177 us (50%)
  waiting for transfers between devices  65 us (19%)
  blocking collectives  58.6 us (17%)
  starting transfers between devices  21.9 us (6%)
  between operations  13.7 us (4%)
  local copies, waits for them, and re-layouts  7.54 us (2%)
    pallas_call x2, Pallas kernels, attention(): pl.pallas_call(functools.partial(attention_kernel, halves), grid=(rows //...  66.5 us
    all_to_all x1, blocking collectives, shards(): lr = lax.all_to_all(lr, AXES, split_axis=0, concat_axis=0, tiled=True)  58.6 us
    pallas_call x1, Pallas kernels, tri_output(): pl.pallas_call(output_kernel, out_shape=(part,) * CHUNKS + (jax.ShapeDtyp...  33 us
    pallas_call x2, Pallas kernels, project(): pl.pallas_call(project_kernel, grid=(rows // group,), out_shape=(shape(co...  28.2 us
    ppermute x2, waiting for transfers between devices, shards(): prev = lax.ppermute(own, 'half', up)  23.6 us
    pallas_call x2, Pallas kernels, project_last(): pl.pallas_call(project_last_kernel, grid=(rows // group,), out_shape=(sha...  20.1 us
    ppermute x2, waiting for transfers between devices, shards(): next_ = lax.ppermute(own, 'half', down)  19.9 us
    all_to_all x1, waiting for transfers between devices, shards(): lax.all_to_all(prod.reshape(width, rows, cols), AXES, split_axis=0, conca...  15.9 us
  transfers between devices with their start and end apart: 9, of which 4 were waited for; matrix products, arithmetic and copies ran while one was open for 0% of the time, Pallas kernels for 17%

profile of v2, /device:TPU:100, one launch (start us, length us, event | category | flops | bytes accessed | tf_op | source)
XLA Modules:
  0.0 346.5 jit_solution(15250950856450675532)
XLA Ops:
  6.5 0.8 convert_convert_fusion
  7.3 0.9 slice.9
  8.2 0.1 copy.15
  8.3 0.7 copy-done.1
  9.0 14.0 %shard_map.82 = bf16[128,2,32,256]{3,2,1,0:T(8,128)(2,1)} custom-call(bf16[32,256,128]{2,1,0:T(8,128)(2,1)} %pair_ref.5, f32[32,256]{1,0:T(8,128)S(1)} %get-tuple-element.44.mask_ref, f32[3,128]{1,0:T(4,128)S(1)} %copy-done.1, bf16[512,128]{1,0:T(8,128)(2,1)S(1)} %bitcast.9), custom_call_target="tpu_custom_call" | custom-call | tf_op jit(solution)/shard_map/pallas_call | solution.py:82
  23.0 58.6 %all_to_all.10 = bf16[128,2,32,256]{3,2,1,0:T(8,128)(2,1)} all-to-all(bf16[128,2,32,256]{3,2,1,0:T(8,128)(2,1)} %shard_map.82), channel_id=1, replica_groups=mesh['rows'=32,'half'=4] {'rows','half'}, dimensions={0} | all-to-all | bytes 8388608 | tf_op jit(solution)/shard_map/all_to_all | solution.py:408
  81.6 6.1 %shard_map.83 = bf16[32,4,32,256]{3,2,1,0:T(8,128)(2,1)} custom-call(bf16[32,4,2,32,256]{4,3,2,1,0:T(8,128)(2,1)} %bitcast.11), custom_call_target="tpu_custom_call" | custom-call | tf_op jit(solution)/shard_map/pallas_call | solution.py:147
  87.7 8.3 %all-to-all-start.1 = ((bf16[128,32,256]{2,1,0:T(8,128)(2,1)}), bf16[128,32,256]{2,1,0:T(8,128)(2,1)S(1)}, u32[]{:S(2)}, u32[]{:S(2)}) async-start(bf16[128,32,256]{2,1,0:T(8,128)(2,1)} %bitcast.12), calls=%async_computation.1 | async-start | bytes 4194304 | tf_op jit(solution)/shard_map/all_to_all | solution.py:411
  96.0 0.8 slice.10.w4_ref
  97.0 9.5 %shard_map.84.gate_ref = bf16[32,256,128]{2,1,0:T(8,128)(2,1)} custom-call(bf16[32,256,128]{2,1,0:T(8,128)(2,1)} %pair_ref.5, f32[3,128]{1,0:T(4,128)S(1)} %copy-done.2, bf16[128,128]{1,0:T(8,128)(2,1)S(1)} %slice.10.w4_ref), custom_call_target="tpu_custom_call" | custom-call | flops 805306368 | bytes 4194304 | tf_op jit(solution)/shard_map/pallas_call | solution.py:107
  106.4 15.9 %all-to-all-done.1.prod_ref = bf16[128,32,256]{2,1,0:T(8,128)(2,1)S(1)} async-done(((bf16[128,32,256]{2,1,0:T(8,128)(2,1)}), bf16[128,32,256]{2,1,0:T(8,128)(2,1)S(1)}, u32[]{:S(2)}, u32[]{:S(2)}) %all-to-all-start.1) | async-done | bytes 2097184 | tf_op jit(solution)/shard_map/all_to_all | solution.py:411
  122.3 1.3 copy-done.10
  123.7 33.0 %shard_map.85 = (bf16[17,256,128]{2,1,0:T(8,128)(2,1)S(1)}, bf16[17,256,128]{2,1,0:T(8,128)(2,1)}, bf16[32,4,256]{2,1,0:T(4,128)(2,1)S(1)}) custom-call(bf16[128,32,256]{2,1,0:T(8,128)(2,1)} %copy-done.10, bf16[32,256,128]{2,1,0:T(8,128)(2,1)} %pair_ref.5, bf16[32,256,128]{2,1,0:T(8,128)(2,1)} %shard_map.84.gate_ref, bf16[64,128]{1,0:T(8,128)(2,1)S(1)} %reshape.44.mask_ref, ...), custom_call_target="tpu_custom_call" | custom-call | tf_op jit(solution)/shard_map/pallas_call | solution.py:195
  156.7 4.6 %collective-permute-start = (bf16[4,32,256]{2,0,1:T(4,128)(2,1)S(1)}, bf16[4,32,256]{2,0,1:T(4,128)(2,1)S(1)}, u32[]{:S(2)}, u32[]{:S(2)}) collective-permute-start(bf16[4,32,256]{2,0,1:T(4,128)(2,1)S(1)} %bitcast.10), channel_id=1, source_target_pairs={{0,0},{1,32},{2,64},{3,96},{4,4},{5,36},{6,68},{7,100},{8,8},{9,40... | collective-permute-start | bytes 196616 | tf_op jit(solution)/shard_map/ppermute | solution.py:427
  161.3 5.6 %collective-permute-done = bf16[4,32,256]{2,0,1:T(4,128)(2,1)S(1)} collective-permute-done((bf16[4,32,256]{2,0,1:T(4,128)(2,1)S(1)}, bf16[4,32,256]{2,0,1:T(4,128)(2,1)S(1)}, u32[]{:S(2)}, u32[]{:S(2)}) %collective-permute-start) | collective-permute-done | bytes 65568 | tf_op jit(solution)/shard_map/ppermute | solution.py:427
  167.0 0.6 copy.14
  167.6 0.6 collective-permute-start.1
  168.2 2.7 collective-permute-start.4
  171.0 2.0 collective-permute-start.6
  172.9 23.6 %collective-permute-done.1.refs_1_.refs_8_ = bf16[17,256,128]{2,1,0:T(8,128)(2,1)} collective-permute-done((bf16[17,256,128]{2,1,0:T(8,128)(2,1)S(1)}, bf16[17,256,128]{2,1,0:T(8,128)(2,1)}, u32[]{:S(2)}, u32[]{:S(2)}) %collective-permute-start.1) | collective-permute-done | bytes 1114144 | tf_op jit(solution)/shard_map/ppermute | solution.py:435
  196.5 3.6 %collective-permute-start.5 = (bf16[17,256,128]{2,1,0:T(8,128)(2,1)S(1)}, bf16[17,256,128]{2,1,0:T(8,128)(2,1)}, u32[]{:S(2)}, u32[]{:S(2)}) collective-permute-start(bf16[17,256,128]{2,1,0:T(8,128)(2,1)S(1)} %collective-permute-done.4.refs_2_.refs_9_), channel_id=1, source_target_pairs={{0,3},{1,0},{2,1},{3,2},{4,7},{5,4},{6,5},{7,6},{8,11},{9,8},{10,9... | collective-permute-start | bytes 3342344 | tf_op jit(solution)/shard_map/ppermute | solution.py:437
  200.2 19.8 %collective-permute-done.3.refs_2_.refs_9_ = bf16[17,256,128]{2,1,0:T(8,128)(2,1)} collective-permute-done((bf16[17,256,128]{2,1,0:T(8,128)(2,1)S(1)}, bf16[17,256,128]{2,1,0:T(8,128)(2,1)}, u32[]{:S(2)}, u32[]{:S(2)}) %collective-permute-start.3) | collective-permute-done | bytes 1114144 | tf_op jit(solution)/shard_map/ppermute | solution.py:436
  220.0 14.1 %shard_map.86 = (bf16[16,256,128]{2,1,0:T(8,128)(2,1)S(1)}, bf16[16,256,128]{2,1,0:T(8,128)(2,1)}, bf16[16,768,128]{2,1,0:T(8,128)(2,1)}, bf16[16,768,128]{2,1,0:T(8,128)(2,1)}, f32[16,8,128]{2,1,0:T(8,128)S(1)}) custom-call(f32[3,128]{1,0:T(4,128)S(1)} %copy-done.2, bf16[128,512]{1,0:T(8,128)(2,1)S(1)} %copy-done.4, bf16[17,256,128]{2,1,0:T(8,128)(2,1)} %copy-done.3, ...), custom_call_target="tpu_custom_call" | custom-call | flops 1610612736 | bytes 12582912 | tf_op jit(solution)/shard_map/pallas_call | solution.py:239
  234.2 1.0 copy-done.13
  235.2 14.1 %shard_map.89 = (bf16[16,256,128]{2,1,0:T(8,128)(2,1)S(1)}, bf16[16,256,128]{2,1,0:T(8,128)(2,1)}, bf16[16,768,128]{2,1,0:T(8,128)(2,1)}, bf16[16,768,128]{2,1,0:T(8,128)(2,1)}, f32[16,8,128]{2,1,0:T(8,128)S(1)}) custom-call(f32[3,128]{1,0:T(4,128)S(1)} %copy-done.2, bf16[128,512]{1,0:T(8,128)(2,1)S(1)} %copy-done.4, ...), custom_call_target="tpu_custom_call" | custom-call | flops 1610612736 | bytes 12582912 | tf_op jit(solution)/shard_map/pallas_call | solution.py:239
  249.3 10.3 %shard_map.87 = (bf16[16,256,128]{2,1,0:T(8,128)(2,1)S(1)}, bf16[16,256,128]{2,1,0:T(8,128)(2,1)}, f32[16,8,128]{2,1,0:T(8,128)S(1)}) custom-call(f32[3,128]{1,0:T(4,128)S(1)} %copy-done.2, bf16[128,512]{1,0:T(8,128)(2,1)S(1)} %copy-done.4, bf16[128,128]{1,0:T(8,128)(2,1)S(1)} %compare_convert_fusion.e_ref, ...), custom_call_target="tpu_custom_call" | custom-call | flops 671088640 | bytes 4194304 | tf_op jit(solution)/shard_map/pallas_call | solution.py:273
  259.6 1.0 copy-done.9
  260.5 9.9 %shard_map.90 = (bf16[16,256,128]{2,1,0:T(8,128)(2,1)S(1)}, bf16[16,256,128]{2,1,0:T(8,128)(2,1)}, f32[16,8,128]{2,1,0:T(8,128)S(1)}) custom-call(f32[3,128]{1,0:T(4,128)S(1)} %copy-done.2, bf16[128,512]{1,0:T(8,128)(2,1)S(1)} %copy-done.4, bf16[128,128]{1,0:T(8,128)(2,1)S(1)} %compare_convert_fusion.e_ref, ...), custom_call_target="tpu_custom_call" | custom-call | flops 671088640 | bytes 4194304 | tf_op jit(solution)/shard_map/pallas_call | solution.py:273
  270.4 1.0 copy-done.8
  271.4 28.5 %shard_map.88 = bf16[16,256,128]{2,1,0:T(8,128)(2,1)S(1)} custom-call(s32[1]{0:T(128)} %bitcast.me_ref, bf16[4,8,4,32,256]{4,3,2,1,0:T(8,128)(2,1)} %bitcast.14, bf16[128,128]{1,0:T(8,128)(2,1)S(1)} %copy-done.5, f32[16,8,128]{2,1,0:T(8,128)S(1)} %get-tuple-element.28.reach_ref, bf16[16,256,128]{2,1,0:T(8,128)(2,1)} %copy-done.7, ...), custom_call_target="tpu_custom_call" | custom-call | flops 34359738368 | bytes 16777216 | tf_op jit(solution)/shard_map/pallas_call | solution.py:379
  299.9 38.1 %shard_map.91 = bf16[16,256,128]{2,1,0:T(8,128)(2,1)S(1)} custom-call(s32[1]{0:T(128)} %bitcast.me_ref, bf16[4,8,4,32,256]{4,3,2,1,0:T(8,128)(2,1)} %bitcast.15, bf16[128,128]{1,0:T(8,128)(2,1)S(1)} %copy-done.5, f32[16,8,128]{2,1,0:T(8,128)S(1)} %get-tuple-element.37.reach_ref, bf16[16,256,128]{2,1,0:T(8,128)(2,1)} %copy-done.6, ...), custom_call_target="tpu_custom_call" | custom-call | flops 34359738368 | bytes 16777216 | tf_op jit(solution)/shard_map/pallas_call | solution.py:379
  338.0 1.5 pad_maximum_fusion
  (38 shorter events, 0.4 us)
Async XLA Ops:
  8.3 0.7 copy-start.1
  87.7 9.1 %copy-start.2 = (f32[3,128]{1,0:T(4,128)S(1)}, f32[3,128]{1,0:T(4,128)}, u32[]{:S(2)}) copy-start(f32[3,128]{1,0:T(4,128)} %gain_ref.13) | copy-start | bytes 4612
  87.7 9.3 %copy-start.11 = (bf16[128,4]{0,1:T(4,128)(2,1)S(1)}, bf16[128,4]{0,1:T(4,128)(2,1)}, u32[]{:S(2)}) copy-start(bf16[128,4]{0,1:T(4,128)(2,1)} %param.14) | copy-start | bytes 3076
  87.7 34.7 %all-to-all-start.1 = ((bf16[128,32,256]{2,1,0:T(8,128)(2,1)}), bf16[128,32,256]{2,1,0:T(8,128)(2,1)S(1)}, u32[]{:S(2)}, u32[]{:S(2)}) async-start(bf16[128,32,256]{2,1,0:T(8,128)(2,1)} %bitcast.12), calls=%async_computation.1 | async-start | bytes 4194304 | tf_op jit(solution)/shard_map/all_to_all | solution.py:411
  96.0 175.4 %all-gather.3.cloned.1.call-start = ((), (), s32[]{:S(2)}) async-start(), calls=%async_computation.2 | async-start | bytes 2162688 | tf_op jit(solution)/shard_map/all_gather | solution.py:428
  97.0 26.7 %copy-start = (bf16[128,128]{1,0:T(8,128)(2,1)S(1)}, bf16[128,128]{1,0:T(8,128)(2,1)}, u32[]{:S(2)}) copy-start(bf16[128,128]{1,0:T(8,128)(2,1)} %wo_ref.3) | copy-start | bytes 98308
  106.4 113.6 %copy-start.4 = (bf16[128,512]{1,0:T(8,128)(2,1)S(1)}, bf16[128,512]{1,0:T(8,128)(2,1)}, u32[]{:S(2)}) copy-start(bf16[128,512]{1,0:T(8,128)(2,1)} %w_ref.7) | copy-start | bytes 393220
  122.3 1.3 copy-start.10
  156.7 63.3 %copy-start.3 = (bf16[17,256,128]{2,1,0:T(8,128)(2,1)}, bf16[17,256,128]{2,1,0:T(8,128)(2,1)S(1)}, u32[]{:S(2)}) copy-start(bf16[17,256,128]{2,1,0:T(8,128)(2,1)S(1)} %get-tuple-element.25.refs_0_.refs_2_.refs_7_) | copy-start | bytes 3342340
  156.7 10.3 %collective-permute-start = (bf16[4,32,256]{2,0,1:T(4,128)(2,1)S(1)}, bf16[4,32,256]{2,0,1:T(4,128)(2,1)S(1)}, u32[]{:S(2)}, u32[]{:S(2)}) collective-permute-start(bf16[4,32,256]{2,0,1:T(4,128)(2,1)S(1)} %bitcast.10), channel_id=1, source_target_pairs={{0,0},{1,32},{2,64},{3,96},{4,4},{5,36},{6,68},{7,100},{8,8},{9,40... | collective-permute-start | bytes 196616 | tf_op jit(solution)/shard_map/ppermute | solution.py:427
  167.6 28.9 %collective-permute-start.1 = (bf16[17,256,128]{2,1,0:T(8,128)(2,1)S(1)}, bf16[17,256,128]{2,1,0:T(8,128)(2,1)}, u32[]{:S(2)}, u32[]{:S(2)}) collective-permute-start(bf16[17,256,128]{2,1,0:T(8,128)(2,1)S(1)} %get-tuple-element.25.refs_0_.refs_2_.refs_7_), channel_id=1, source_target_pairs={{0,1},{1,2},{2,3},{3,0},{4,5},{5,6},{6,7},{7,4},{8,9},{9,10},{10,1... | collective-permute-start | bytes 3342344 | tf_op jit(solution)/shard_map/ppermute | solution.py:435
  168.2 28.3 %collective-permute-start.4 = (bf16[17,256,128]{2,1,0:T(8,128)(2,1)}, bf16[17,256,128]{2,1,0:T(8,128)(2,1)S(1)}, u32[]{:S(2)}, u32[]{:S(2)}) collective-permute-start(bf16[17,256,128]{2,1,0:T(8,128)(2,1)} %get-tuple-element.34.refs_0_.refs_2_.refs_7_), channel_id=1, source_target_pairs={{0,3},{1,0},{2,1},{3,2},{4,7},{5,4},{6,5},{7,6},{8,11},{9,8},{10,9... | collective-permute-start | bytes 3342344 | tf_op jit(solution)/shard_map/ppermute | solution.py:436
  170.9 49.1 %collective-permute-start.3 = (bf16[17,256,128]{2,1,0:T(8,128)(2,1)S(1)}, bf16[17,256,128]{2,1,0:T(8,128)(2,1)}, u32[]{:S(2)}, u32[]{:S(2)}) collective-permute-start(bf16[17,256,128]{2,1,0:T(8,128)(2,1)S(1)} %get-tuple-element.25.refs_0_.refs_2_.refs_7_), channel_id=1, source_target_pairs={{0,3},{1,0},{2,1},{3,2},{4,7},{5,4},{6,5},{7,6},{8,11},{9,8},{10,9... | collective-permute-start | bytes 3342344 | tf_op jit(solution)/shard_map/ppermute | solution.py:436
  171.0 63.2 %collective-permute-start.6 = (bf16[17,256,128]{2,1,0:T(8,128)(2,1)}, bf16[17,256,128]{2,1,0:T(8,128)(2,1)S(1)}, u32[]{:S(2)}, u32[]{:S(2)}) collective-permute-start(bf16[17,256,128]{2,1,0:T(8,128)(2,1)} %get-tuple-element.34.refs_0_.refs_2_.refs_7_), channel_id=1, source_target_pairs={{0,1},{1,2},{2,3},{3,0},{4,5},{5,6},{6,7},{7,4},{8,9},{9,10},{10,1... | collective-permute-start | bytes 3342344 | tf_op jit(solution)/shard_map/ppermute | solution.py:435
  196.5 52.8 %collective-permute-start.2 = (bf16[17,256,128]{2,1,0:T(8,128)(2,1)}, bf16[17,256,128]{2,1,0:T(8,128)(2,1)}, u32[]{:S(2)}, u32[]{:S(2)}) collective-permute-start(bf16[17,256,128]{2,1,0:T(8,128)(2,1)} %collective-permute-done.1.refs_1_.refs_8_), channel_id=1, source_target_pairs={{0,1},{1,2},{2,3},{3,0},{4,5},{5,6},{6,7},{7,4},{8,9},{9,10},{10,1... | collective-permute-start | bytes 3342344 | tf_op jit(solution)/shard_map/ppermute | solution.py:437
  196.5 37.7 %copy-start.12 = (bf16[17,256,128]{2,1,0:T(8,128)(2,1)}, bf16[17,256,128]{2,1,0:T(8,128)(2,1)S(1)}, u32[]{:S(2)}) copy-start(bf16[17,256,128]{2,1,0:T(8,128)(2,1)S(1)} %collective-permute-done.4.refs_2_.refs_9_) | copy-start | bytes 3342340
  196.5 64.0 %collective-permute-start.5 = (bf16[17,256,128]{2,1,0:T(8,128)(2,1)S(1)}, bf16[17,256,128]{2,1,0:T(8,128)(2,1)}, u32[]{:S(2)}, u32[]{:S(2)}) collective-permute-start(bf16[17,256,128]{2,1,0:T(8,128)(2,1)S(1)} %collective-permute-done.4.refs_2_.refs_9_), channel_id=1, source_target_pairs={{0,3},{1,0},{2,1},{3,2},{4,7},{5,4},{6,5},{7,6},{8,11},{9,8},{10,9... | collective-permute-start | bytes 3342344 | tf_op jit(solution)/shard_map/ppermute | solution.py:437
  234.2 15.1 %copy-start.7 = (bf16[16,256,128]{2,1,0:T(8,128)(2,1)}, bf16[16,256,128]{2,1,0:T(8,128)(2,1)S(1)}, u32[]{:S(2)}) copy-start(bf16[16,256,128]{2,1,0:T(8,128)(2,1)S(1)} %get-tuple-element.26.q_ref.refs_0_) | copy-start | bytes 3145732
  234.2 1.0 copy-start.13
  249.3 11.3 %copy-start.6 = (bf16[16,256,128]{2,1,0:T(8,128)(2,1)}, bf16[16,256,128]{2,1,0:T(8,128)(2,1)S(1)}, u32[]{:S(2)}) copy-start(bf16[16,256,128]{2,1,0:T(8,128)(2,1)S(1)} %get-tuple-element.35.q_ref.refs_0_) | copy-start | bytes 3145732
  249.3 22.1 %copy-start.5 = (bf16[128,128]{1,0:T(8,128)(2,1)S(1)}, bf16[128,128]{1,0:T(8,128)(2,1)}, u32[]{:S(2)}) copy-start(bf16[128,128]{1,0:T(8,128)(2,1)} %wo_ref.5) | copy-start | bytes 98308
  259.6 1.0 copy-start.9
  270.4 1.0 copy-start.8
Sparse Core Ops, SparseCore 0:
  167.7 40.6 all-gather.2
